TPU v7x, 32 devices: a whole 2x2x4 slice. The times are simulated.
32 devices in a mesh: sym: 4 (over y, core), rows: 8 (over z, x).
Axes of the slice: x: 2, y: 2, z: 4, core: 2. Of those that a mesh axis runs over, the one named last changes fastest.
Arguments:
- coeffs: bfloat16 [4096, 4096], P('rows', 'sym'), may hold values from -6 to 6
- beta_op: bfloat16 [4, 1024, 1024], P('sym'), may hold values from -0.1875 to 0.1875
- mix_op: bfloat16 [4, 4, 8, 128, 128], P('sym'), may hold values from -0.125 to 0.125
- pair_op: bfloat16 [8, 128, 128], replicated, may hold values from -0.1875 to 0.1875
- send_list: int32 [8, 8, 2], replicated, may hold values from -1 to 3, as said below
- mix_slot: int32 [32, 16], replicated, may hold values from 0 to 15, as said below
- mix_sign: int32 [32, 16], replicated, may hold values from 0 to 1
- mix_pair: int32 [32, 16], replicated, may hold values from 0 to 3
- aa_src: int32 [32, 8], replicated, may hold values from 0 to 31
- aa_sign: int32 [32, 8], replicated, may hold values from 0 to 1
- aa_pair: int32 [32, 8], replicated, may hold values from 0 to 7
Outputs:
- sigma: float32 [4096, 4096], P('rows', 'sym')
Inputs may be any that keep to these rules, and one draw needn't show every extreme that they name: send_list[s, r, c] is the block, counted within device s's own 4 alpha blocks, that s sends to device r in slot c, or -1 for an empty slot; live slots of a pair come first and hold distinct blocks; every device sends at least one block to itself; in every draw some device receives 2 blocks from every device. mix_slot[P, l] = s * 2 + c names slot c of send_list[s, P // 4], always a live one; every live slot sent to a device is named by some entry of that device's destination blocks.
All inputs are finite; a program needn't handle non-finite values.
Results may differ from a plain program's by a relative error of at most 0.0075.
Values may be sent and summed in bfloat16 or wider, within the bound.
A program may use at most 128 MiB of HBM per device.

v0:
```python
import jax
import jax.numpy as jnp
from jax import lax
from jax.sharding import PartitionSpec as P

TILE = 128
BT = 8
ABLK = 4
CAP = 2
NPA = 8


def per_device(
    coeffs,
    beta_op,
    mix_op,
    pair_op,
    send_list,
    mix_slot,
    mix_sign,
    mix_pair,
    aa_src,
    aa_sign,
    aa_pair,
):
    rows_here, beta_here = coeffs.shape
    sectors = lax.axis_size("sym")
    rank_count = lax.axis_size("rows")
    sector = lax.axis_index("sym")
    my_rank = lax.axis_index("rows")
    block_count = aa_src.shape[0]
    total_rows = block_count * TILE
    col_width = beta_here // rank_count
    local_term = jnp.dot(coeffs, beta_op[0], preferred_element_type=jnp.float32)
    flipped = coeffs.T
    columns = lax.all_to_all(flipped, "rows", split_axis=0, concat_axis=1, tiled=True)
    col_blocks = columns.reshape(col_width, block_count, TILE)
    picked = jnp.take(col_blocks, aa_src, axis=1)
    operator_ids = jnp.arange(NPA, dtype=jnp.int32)
    aa_weight = (
        (1 - 2 * aa_sign)[:, :, None]
        * (aa_pair[:, :, None] == operator_ids[None, None, :]).astype(jnp.int32)
    ).astype(jnp.bfloat16)
    combined = jnp.einsum(
        "cpki,pkg->cpgi", picked, aa_weight, preferred_element_type=jnp.float32
    ).astype(jnp.bfloat16)
    alpha_part = jnp.einsum(
        "cpgj,gij->cpi", combined, pair_op, preferred_element_type=jnp.float32
    ).reshape(col_width, total_rows)
    returned = lax.all_to_all(
        alpha_part.astype(jnp.bfloat16), "rows", split_axis=1, concat_axis=0, tiled=True
    ).astype(alpha_part.dtype)
    dest_ids = jnp.arange(sectors, dtype=jnp.int32)
    pair_of = jnp.bitwise_xor(sector, dest_ids)
    operators = jnp.take(mix_op[0], pair_of, axis=0)
    sign_all = (1 - 2 * mix_sign).astype(jnp.float32)
    my_sends = lax.dynamic_index_in_dim(send_list, my_rank, 0, keepdims=False)
    blocks = coeffs.reshape(ABLK, TILE, beta_here)
    taken = jnp.take(blocks, jnp.maximum(my_sends, 0), axis=0)
    outgoing = jnp.where((my_sends >= 0)[:, :, None, None], taken, jnp.zeros_like(taken))
    arrived = lax.all_to_all(outgoing, "rows", split_axis=0, concat_axis=0, tiled=True)
    slot_total = rank_count * CAP
    arrived = arrived.reshape(slot_total, TILE * beta_here)
    my_slots = lax.dynamic_slice_in_dim(mix_slot, my_rank * ABLK, ABLK, 0)
    my_signs = lax.dynamic_slice_in_dim(sign_all, my_rank * ABLK, ABLK, 0)
    my_pairs = lax.dynamic_slice_in_dim(mix_pair, my_rank * ABLK, ABLK, 0)
    weight = my_signs[None, :, :] * (my_pairs[None, :, :] == pair_of[:, None, None]).astype(
        jnp.float32
    )
    onehot = (
        my_slots[:, :, None] == jnp.arange(slot_total, dtype=jnp.int32)[None, None, :]
    ).astype(jnp.float32)
    mixing = (
        jnp.einsum("dpl,pls->dps", weight, onehot)
        .astype(jnp.bfloat16)
        .reshape(sectors * ABLK, slot_total)
    )
    inputs = jnp.dot(mixing, arrived, preferred_element_type=jnp.float32).astype(jnp.bfloat16)
    inputs = inputs.reshape(sectors, rows_here, BT, TILE)
    contract_eq = "drtk,dtkj->drtj"
    row_count = lax.axis_size("sym") * rows_here
    products = jnp.einsum(contract_eq, inputs, operators, preferred_element_type=jnp.float32)
    mixed = lax.psum_scatter(
        products.reshape(row_count, beta_here).astype(jnp.bfloat16),
        "sym",
        scatter_dimension=0,
        tiled=True,
    ).astype(jnp.float32)
    return local_term + returned.T + mixed


def solution(mesh):
    in_specs = (
        P("rows", "sym"),
        P("sym", None, None),
        P("sym", None, None, None, None),
        P(),
        P(),
        P(),
        P(),
        P(),
        P(),
        P(),
        P(),
    )
    out_specs = P("rows", "sym")
    return jax.shard_map(
        per_device, mesh=mesh, in_specs=in_specs, out_specs=out_specs, check_vma=False
    )
```

profile of v0, /device:TPU:10, one launch (start us, length us, event | category | flops | bytes accessed | tf_op | source)
XLA Modules:
  0.0 247.4 jit_solution(11930271022779355826)
XLA Ops:
  6.5 0.8 compare_bitcast_fusion
  7.4 0.1 copy.76
  7.5 0.1 copy.75
  7.6 0.1 copy.77
  7.6 0.1 reshape.117
  7.7 4.0 %gather_fusion.2 = bf16[16,128,1024]{2,1,0:T(8,128)(2,1)} fusion(bf16[4,128,1024]{2,1,0:T(8,128)(2,1)} %bitcast.72, s32[1024]{0:T(1024)S(1)} %pad_clamp_fusion), kind=kCustom, calls=%fused_computation.2 | custom fusion | bytes 8388672 | tf_op jit(solution)/shard_map/jit(_take)/gather | solution.py:59
  11.8 4.7 %select_select_fusion = bf16[8,2,128,1024]{3,2,1,0:T(8,128)(2,1)} fusion(bf16[8,2,128,1024]{3,2,1,0:T(8,128)(2,1)} %bitcast.74, pred[8,2]{1,0:T(8,128)(4,1)S(1)} %copy.76, pred[8,2]{1,0:T(8,128)(4,1)S(1)} %copy.75), kind=kLoop, calls=%fused_computation.16 | loop fusion | flops 4194304 | bytes 8388640 | tf_op jit(solution)/shard_map/jit(_where)/select_n | solution.py:60
  16.5 6.4 %all-to-all-start.2 = ((bf16[8,2,128,1024]{3,2,1,0:T(8,128)(2,1)}), bf16[8,2,128,1024]{3,2,1,0:T(8,128)(2,1)}, u32[]{:S(2)}, u32[]{:S(2)}) async-start(bf16[8,2,128,1024]{3,2,1,0:T(8,128)(2,1)} %select_select_fusion), calls=%async_computation.2 | async-start | bytes 8388608 | tf_op jit(solution)/shard_map/all_to_all | solution.py:61
  22.9 0.1 copy.71
  23.1 0.1 copy.73
  23.2 0.2 fusion.20
  23.5 2.0 gather_fusion.1
  25.5 87.2 %all-to-all-done.2 = bf16[8,2,128,1024]{3,2,1,0:T(8,128)(2,1)} async-done(((bf16[8,2,128,1024]{3,2,1,0:T(8,128)(2,1)}), bf16[8,2,128,1024]{3,2,1,0:T(8,128)(2,1)}, u32[]{:S(2)}, u32[]{:S(2)}) %all-to-all-start.2) | async-done | bytes 4194336 | tf_op jit(solution)/shard_map/all_to_all | solution.py:61
  112.7 4.5 %copy.85 = bf16[2,8,128,1024]{3,1,2,0:T(8,128)(2,1)S(1)} copy(bf16[2,8,128,1024]{3,2,1,0:T(8,128)(2,1)} %bitcast.30) | data formatting | bytes 8388608
  117.2 3.2 %convolution_convert_fusion = bf16[16,131072]{1,0:T(8,128)(2,1)} fusion(bf16[16,16]{1,0:T(8,128)(2,1)S(1)} %bitcast.82, bf16[16,131072]{1,0:T(8,128)(2,1)S(1)} %bitcast.71), kind=kOutput, calls=%fused_computation.3 | convolution fusion | flops 69206016 | bytes 8389120 | tf_op jit(solution)/shard_map/dot_general | solution.py:78
  120.4 4.8 %reshape.97 = bf16[4,512,8,128]{3,2,1,0:T(8,128)(2,1)} reshape(bf16[16,131072]{1,0:T(8,128)(2,1)} %convolution_convert_fusion) | data formatting | bytes 8388608 | tf_op jit(solution)/shard_map/reshape | solution.py:79
  125.3 5.7 %convert_bitcast_fusion.1 = bf16[4,512,8,128]{1,3,2,0:T(8,128)(2,1)} fusion(bf16[4,512,8,128]{3,2,1,0:T(8,128)(2,1)} %reshape.97, bf16[4,8,128,128]{3,2,1,0:T(8,128)(2,1)S(1)} %gather_fusion.1, pred[4]{0:T(512)(128)(4,1)S(1)} %compare_and_fusion.1), kind=kOutput, calls=%fused_computation.15 | convolution fusion | flops 539492352 | bytes 9437188 | tf_op jit(solution)/shard_map/drtk,dtkj->drtj/dot_general | solution.py:82
  130.9 7.5 %copy.80 = bf16[4,512,8,128]{3,2,1,0:T(8,128)(2,1)} copy(bf16[4,512,8,128]{1,3,2,0:T(8,128)(2,1)} %convert_bitcast_fusion.1) | data formatting | bytes 8388608 | tf_op jit(solution)/shard_map/convert_element_type | solution.py:84
  138.4 5.2 %copy.103 = bf16[256,8,8,128]{3,1,2,0:T(8,128)(2,1)} copy(bf16[256,8,8,128]{3,2,1,0:T(8,128)(2,1)} %bitcast.75) | data formatting | bytes 8388608
  143.7 1.2 copy-done.1
  144.9 1.3 copy.64
  146.2 7.0 %all-to-all-start = ((bf16[8,128,512]{2,1,0:T(8,128)(2,1)}), bf16[8,128,512]{2,1,0:T(8,128)(2,1)S(1)}, u32[]{:S(2)}, u32[]{:S(2)}) async-start(bf16[8,128,512]{2,1,0:T(8,128)(2,1)} %bitcast.78), calls=%async_computation | async-start | bytes 2097152 | tf_op jit(solution)/shard_map/all_to_all | solution.py:36
  153.2 0.1 copy.63
  153.4 0.1 reshape.101
  153.7 22.2 %all-to-all-done = bf16[8,128,512]{2,1,0:T(8,128)(2,1)S(1)} async-done(((bf16[8,128,512]{2,1,0:T(8,128)(2,1)}), bf16[8,128,512]{2,1,0:T(8,128)(2,1)S(1)}, u32[]{:S(2)}, u32[]{:S(2)}) %all-to-all-start) | async-done | bytes 1048608 | tf_op jit(solution)/shard_map/all_to_all | solution.py:36
  175.9 1.3 copy.65
  177.2 1.6 copy.67
  178.8 8.6 %gather_fusion = bf16[256,128,128]{2,1,0:T(8,128)(2,1)} fusion(bf16[128,32,128]{2,0,1:T(8,128)(2,1)S(1)} %copy.67, s32[1024]{0:T(1024)S(1)} %pad_clamp_fusion.2), kind=kCustom, calls=%fused_computation | custom fusion | bytes 16778240 | tf_op jit(solution)/shard_map/jit(_take)/gather | solution.py:38
  187.5 12.0 %convert_bitcast_fusion = bf16[128,32,8,128]{3,2,0,1:T(8,128)(2,1)} fusion(bf16[32,8,128,128]{3,2,1,0:T(8,128)(2,1)} %bitcast.76, pred[32,8]{1,0:T(8,128)(4,1)S(1)} %copy.63, s32[32,8]{1,0:T(8,128)S(1)} %copy.62, s32[32,8]{1,0:T(8,128)S(1)} %copy.61), kind=kOutput, calls=%fused_computation.9 | convolution fusion | flops 75503616 | bytes 16779520 | tf_op jit(solution)/shard_map/cpki,pkg->cpgi/dot_general | solution.py:44
  199.5 6.4 %bitcast_convert_fusion = bf16[128,32,128]{0,2,1:T(8,128)(2,1)S(1)} fusion(bf16[128,32,8,128]{3,2,0,1:T(8,128)(2,1)} %convert_bitcast_fusion, bf16[8,128,128]{2,1,0:T(8,128)(2,1)S(1)} %copy-done.9), kind=kOutput, calls=%fused_computation.20 | convolution fusion | flops 1074266112 | bytes 9699328 | tf_op jit(solution)/shard_map/cpgj,gij->cpi/dot_general | solution.py:47
  205.9 30.6 %all_to_all.31 = bf16[128,8,512]{0,2,1:T(8,128)(2,1)} all-to-all(bf16[128,8,512]{0,2,1:T(8,128)(2,1)S(1)} %bitcast.81), channel_id=1, replica_groups=mesh['sym'=4,'rows'=8] {'rows'}, dimensions={1} | all-to-all | bytes 2097152 | tf_op jit(solution)/shard_map/all_to_all | solution.py:50
  236.5 4.1 %fusion.13 = f32[512,1024]{1,0:T(8,128)} fusion(bf16[512,1024]{1,0:T(8,128)(2,1)} %reduce-scatter.2.cloned.1.call-done, bf16[512,1024]{1,0:T(8,128)(2,1)S(1)} %copy-done.2, bf16[1,1024,1024]{2,1,0:T(8,128)(2,1)S(1)} %copy-done, bf16[128,8,512]{0,2,1:T(8,128)(2,1)} %all_to_all.31), kind=kOutput, calls=%fused_computation.19 | convolution fusion | flops 1075838976 | bytes 7340032 | tf_op jit(solution)/shard_map/dot_general | solution.py:34
  (38 shorter events, 0.6 us)
Async XLA Ops:
  6.5 229.9 %copy-start = (bf16[1,1024,1024]{2,1,0:T(8,128)(2,1)S(1)}, bf16[1,1024,1024]{2,1,0:T(8,128)(2,1)}, u32[]{:S(2)}) copy-start(bf16[1,1024,1024]{2,1,0:T(8,128)(2,1)} %param.12) | copy-start | bytes 6291460
  16.4 6.4 %copy-start.6 = (s32[32,16]{0,1:T(8,128)S(1)}, s32[32,16]{0,1:T(8,128)}, u32[]{:S(2)}) copy-start(s32[32,16]{0,1:T(8,128)} %param.16) | copy-start | bytes 6148
  16.4 6.5 %copy-start.4 = (s32[32,16]{0,1:T(8,128)S(1)}, s32[32,16]{0,1:T(8,128)}, u32[]{:S(2)}) copy-start(s32[32,16]{0,1:T(8,128)} %param.17) | copy-start | bytes 6148
  16.4 6.5 %copy-start.5 = (s32[32,16]{0,1:T(8,128)S(1)}, s32[32,16]{0,1:T(8,128)}, u32[]{:S(2)}) copy-start(s32[32,16]{0,1:T(8,128)} %param.18) | copy-start | bytes 6148
  16.5 96.3 %all-to-all-start.2 = ((bf16[8,2,128,1024]{3,2,1,0:T(8,128)(2,1)}), bf16[8,2,128,1024]{3,2,1,0:T(8,128)(2,1)}, u32[]{:S(2)}, u32[]{:S(2)}) async-start(bf16[8,2,128,1024]{3,2,1,0:T(8,128)(2,1)} %select_select_fusion), calls=%async_computation.2 | async-start | bytes 8388608 | tf_op jit(solution)/shard_map/all_to_all | solution.py:61
  22.8 213.7 %reduce-scatter.2.cloned.1.call-start = ((), (), s32[]{:S(2)}) async-start(), calls=%async_computation.4 | async-start | bytes 5242880 | tf_op jit(solution)/shard_map/reduce_scatter | solution.py:83
  143.7 1.2 copy-start.1
  143.7 9.6 %copy-start.3 = (s32[32,8]{0,1:T(8,128)S(1)}, s32[32,8]{0,1:T(8,128)}, u32[]{:S(2)}) copy-start(s32[32,8]{0,1:T(8,128)} %param.19) | copy-start | bytes 3076
  143.7 9.8 %copy-start.8 = (s32[32,8]{0,1:T(8,128)S(1)}, s32[32,8]{0,1:T(8,128)}, u32[]{:S(2)}) copy-start(s32[32,8]{0,1:T(8,128)} %param.20) | copy-start | bytes 3076
  143.7 9.9 %copy-start.7 = (s32[32,8]{0,1:T(8,128)S(1)}, s32[32,8]{0,1:T(8,128)}, u32[]{:S(2)}) copy-start(s32[32,8]{0,1:T(8,128)} %param.21) | copy-start | bytes 3076
  146.2 29.7 %all-to-all-start = ((bf16[8,128,512]{2,1,0:T(8,128)(2,1)}), bf16[8,128,512]{2,1,0:T(8,128)(2,1)S(1)}, u32[]{:S(2)}, u32[]{:S(2)}) async-start(bf16[8,128,512]{2,1,0:T(8,128)(2,1)} %bitcast.78), calls=%async_computation | async-start | bytes 2097152 | tf_op jit(solution)/shard_map/all_to_all | solution.py:36
  187.5 12.0 %copy-start.9 = (bf16[8,128,128]{2,1,0:T(8,128)(2,1)S(1)}, bf16[8,128,128]{2,1,0:T(8,128)(2,1)}, u32[]{:S(2)}) copy-start(bf16[8,128,128]{2,1,0:T(8,128)(2,1)} %param.14) | copy-start | bytes 786436
  199.5 37.0 %copy-start.2 = (bf16[512,1024]{1,0:T(8,128)(2,1)S(1)}, bf16[512,1024]{1,0:T(8,128)(2,1)}, u32[]{:S(2)}) copy-start(bf16[512,1024]{1,0:T(8,128)(2,1)} %param.11) | copy-start | bytes 3145732
Sparse Core Ops, SparseCore 0:
  143.8 46.4 reduce-scatter.1
where the time goes:
time: 251 us; the launch traced here: 247 us
  waiting for transfers between devices  109 us (43%)
  local copies, waits for them, and re-layouts  43.3 us (17%)
  matrix products  31.6 us (13%)
  blocking collectives  30.6 us (12%)
  between operations  13.5 us (5%)
  starting transfers between devices  13.4 us (5%)
  other arithmetic  5.65 us (2%)
    all_to_all x1, waiting for transfers between devices, per_device(): lax.all_to_all(outgoing, 'rows', split_axis=0, concat_axis=0, tiled=True)  87.2 us
    all_to_all x1, blocking collectives, per_device(): lax.all_to_all(alpha_part.astype(jnp.bfloat16), 'rows', split_axis=1, con...  30.6 us
    all_to_all x1, waiting for transfers between devices, per_device(): lax.all_to_all(flipped, 'rows', split_axis=0, concat_axis=1, tiled=True)  22.2 us
    unnamed x24, local copies, waits for them, and re-layouts  12.4 us
    dot_general x1, matrix products, per_device(): jnp.einsum('cpki,pkg->cpgi', picked, aa_weight, preferred_element_type=jn...  12 us
    gather x1, local copies, waits for them, and re-layouts, per_device(): picked = jnp.take(col_blocks, aa_src, axis=1)  8.63 us
    convert_element_type x1, local copies, waits for them, and re-layouts, per_device(): products.reshape(row_count, beta_here).astype(jnp.bfloat16)  7.52 us
    all_to_all x1, starting transfers between devices, per_device(): lax.all_to_all(flipped, 'rows', split_axis=0, concat_axis=1, tiled=True)  7.02 us
  transfers between devices with their start and end apart: 3, of which 2 were waited for; matrix products, arithmetic and copies ran while one was open for 14% of the time, Pallas kernels for 0%

commit v1 on v0

--- a/solution.py
+++ b/solution.py
@@ -1,16 +1,21 @@
+import functools
+
 import jax
 import jax.numpy as jnp
 from jax import lax
+from jax.experimental import pallas as pl
+from jax.experimental.pallas import tpu as pltpu
 from jax.sharding import PartitionSpec as P
 
 TILE = 128
 BT = 8
-ABLK = 4
 CAP = 2
 NPA = 8
-
-
-def per_device(
+CHUNK = 32
+MESH = pl.DeviceIdType.MESH
+
+
+def spread(
     coeffs,
     beta_op,
     mix_op,
@@ -24,6 +29,7 @@
     aa_pair,
 ):
     rows_here, beta_here = coeffs.shape
+    ablk = rows_here // TILE
     sectors = lax.axis_size("sym")
     rank_count = lax.axis_size("rows")
     sector = lax.axis_index("sym")
@@ -55,15 +61,15 @@
     operators = jnp.take(mix_op[0], pair_of, axis=0)
     sign_all = (1 - 2 * mix_sign).astype(jnp.float32)
     my_sends = lax.dynamic_index_in_dim(send_list, my_rank, 0, keepdims=False)
-    blocks = coeffs.reshape(ABLK, TILE, beta_here)
+    blocks = coeffs.reshape(ablk, TILE, beta_here)
     taken = jnp.take(blocks, jnp.maximum(my_sends, 0), axis=0)
     outgoing = jnp.where((my_sends >= 0)[:, :, None, None], taken, jnp.zeros_like(taken))
     arrived = lax.all_to_all(outgoing, "rows", split_axis=0, concat_axis=0, tiled=True)
     slot_total = rank_count * CAP
     arrived = arrived.reshape(slot_total, TILE * beta_here)
-    my_slots = lax.dynamic_slice_in_dim(mix_slot, my_rank * ABLK, ABLK, 0)
-    my_signs = lax.dynamic_slice_in_dim(sign_all, my_rank * ABLK, ABLK, 0)
-    my_pairs = lax.dynamic_slice_in_dim(mix_pair, my_rank * ABLK, ABLK, 0)
+    my_slots = lax.dynamic_slice_in_dim(mix_slot, my_rank * ablk, ablk, 0)
+    my_signs = lax.dynamic_slice_in_dim(sign_all, my_rank * ablk, ablk, 0)
+    my_pairs = lax.dynamic_slice_in_dim(mix_pair, my_rank * ablk, ablk, 0)
     weight = my_signs[None, :, :] * (my_pairs[None, :, :] == pair_of[:, None, None]).astype(
         jnp.float32
     )
@@ -73,15 +79,15 @@
     mixing = (
         jnp.einsum("dpl,pls->dps", weight, onehot)
         .astype(jnp.bfloat16)
-        .reshape(sectors * ABLK, slot_total)
+        .reshape(sectors * ablk, slot_total)
     )
     inputs = jnp.dot(mixing, arrived, preferred_element_type=jnp.float32).astype(jnp.bfloat16)
     inputs = inputs.reshape(sectors, rows_here, BT, TILE)
-    contract_eq = "drtk,dtkj->drtj"
-    row_count = lax.axis_size("sym") * rows_here
-    products = jnp.einsum(contract_eq, inputs, operators, preferred_element_type=jnp.float32)
+    products = jnp.einsum(
+        "drtk,dtkj->drtj", inputs, operators, preferred_element_type=jnp.float32
+    )
     mixed = lax.psum_scatter(
-        products.reshape(row_count, beta_here).astype(jnp.bfloat16),
+        products.reshape(sectors * rows_here, beta_here).astype(jnp.bfloat16),
         "sym",
         scatter_dimension=0,
         tiled=True,
@@ -89,21 +95,342 @@
     return local_term + returned.T + mixed
 
 
+def kernel(
+    ranks,
+    coeffs,
+    beta_op,
+    mix_op,
+    pair_op,
+    mix_src,
+    mix_weight,
+    aa_src,
+    aa_op,
+    out,
+    cols,
+    mine,
+    beta,
+    pairs,
+    mops,
+    combo,
+    base,
+    across,
+    core_out,
+    core_in,
+    y_out,
+    y_in,
+    back_out,
+    back_in,
+    local_sem,
+    go_send,
+    go_recv,
+    core_send,
+    core_recv,
+    y_send,
+    y_recv,
+    back_send,
+    back_recv,
+):
+    ablk, _, beta_here = coeffs.shape
+    entries = mix_src.shape[1]
+    ka = aa_src.shape[1]
+    npa = pair_op.shape[0]
+    me = lax.axis_index("rows")
+    sym = lax.axis_index("sym")
+    core_mate = sym + 1 - 2 * lax.rem(sym, 2)
+    y_mate = lax.rem(sym + 2, 4)
+
+    def block_cols(r):
+        return pl.ds(pl.multiple_of(r * TILE, TILE), TILE)
+
+    def blocks_of(r):
+        return pl.ds(r * ablk, ablk)
+
+    load_mine = pltpu.make_async_copy(coeffs, mine, local_sem.at[0])
+    load_beta = pltpu.make_async_copy(beta_op.at[0], beta, local_sem.at[1])
+    load_mops = pltpu.make_async_copy(mix_op.at[0, :, me], mops, local_sem.at[2])
+    load_own = pltpu.make_async_copy(
+        coeffs.at[:, :, block_cols(me)], cols.at[blocks_of(me)], local_sem.at[3]
+    )
+    load_mine.start()
+    load_beta.start()
+    load_mops.start()
+    load_own.start()
+
+    barrier = pltpu.get_barrier_semaphore()
+    for i in range(1, ranks):
+        pl.semaphore_signal(
+            barrier, inc=1, device_id={"rows": lax.rem(me + i, ranks)}, device_id_type=MESH
+        )
+    pl.semaphore_signal(barrier, inc=1, device_id={"sym": core_mate}, device_id_type=MESH)
+    pl.semaphore_signal(barrier, inc=1, device_id={"sym": y_mate}, device_id_type=MESH)
+    pl.semaphore_wait(barrier, ranks + 1)
+
+    def go(i):
+        r = lax.rem(me + 1 + i, ranks)
+        return pltpu.make_async_remote_copy(
+            src_ref=coeffs.at[:, :, block_cols(r)],
+            dst_ref=cols.at[blocks_of(me)],
+            send_sem=go_send.at[i],
+            recv_sem=go_recv.at[i],
+            device_id={"rows": r},
+            device_id_type=MESH,
+        )
+
+    def go_in(i):
+        r = lax.rem(me + 2 * ranks - 1 - i, ranks)
+        return pltpu.make_async_remote_copy(
+            src_ref=coeffs.at[:, :, block_cols(r)],
+            dst_ref=cols.at[blocks_of(r)],
+            send_sem=go_send.at[i],
+            recv_sem=go_recv.at[i],
+            device_id={"rows": r},
+            device_id_type=MESH,
+        )
+
+    for i in range(ranks - 1):
+        go(i).start()
+
+    for k in range(npa):
+        pairs[k] = pair_op[k]
+        pairs[npa + k] = -pair_op[k]
+
+    load_mine.wait()
+    load_beta.wait()
+    width = 2 * TILE
+
+    @pl.loop(0, beta_here // width)
+    def _(n):
+        at = pl.ds(pl.multiple_of(n * width, width), width)
+
+        for m in range(ablk):
+            out[m, :, at] = jnp.dot(
+                mine[m], beta[:, at], preferred_element_type=jnp.float32
+            )
+
+    load_mops.wait()
+    load_own.wait()
+    for i in range(ranks - 1):
+        go_in(i).wait_recv()
+    for i in range(ranks - 1):
+        go(i).wait_send()
+
+    def core_copy(i):
+        return pltpu.make_async_remote_copy(
+            src_ref=core_out.at[i],
+            dst_ref=core_in.at[i],
+            send_sem=core_send.at[i],
+            recv_sem=core_recv.at[i],
+            device_id={"sym": core_mate},
+            device_id_type=MESH,
+        )
+
+    def y_copy(i):
+        return pltpu.make_async_remote_copy(
+            src_ref=y_out.at[i],
+            dst_ref=y_in.at[i],
+            send_sem=y_send.at[i],
+            recv_sem=y_recv.at[i],
+            device_id={"sym": y_mate},
+            device_id_type=MESH,
+        )
+
+    def back_copy(i):
+        return pltpu.make_async_remote_copy(
+            src_ref=back_out.at[i],
+            dst_ref=back_in.at[i],
+            send_sem=back_send.at[i],
+            recv_sem=back_recv.at[i],
+            device_id={"rows": lax.rem(me + 1 + i, ranks)},
+            device_id_type=MESH,
+        )
+
+    def compute(i):
+        r = lax.rem(me + 1 + i, ranks)
+
+        def one(b, carry):
+            p = r * ablk + b
+            alpha = jnp.dot(
+                jnp.concatenate([pairs[aa_op[p, k]] for k in range(ka)], axis=1),
+                jnp.concatenate([cols[aa_src[p, k]] for k in range(ka)], axis=0),
+                preferred_element_type=jnp.float32,
+            )
+            sources = [mix_src[p, l] for l in range(entries)]
+            for c in range(TILE // CHUNK):
+                total = [jnp.zeros((CHUNK, TILE), jnp.float32) for _ in range(4)]
+                for l in range(entries):
+                    x = cols[sources[l], c * CHUNK : (c + 1) * CHUNK, :].astype(jnp.float32)
+                    for g in range(4):
+                        total[g] = total[g] + mix_weight[p, g * entries + l] * x
+                for g in range(4):
+                    combo[g, c * CHUNK : (c + 1) * CHUNK, :] = total[g].astype(jnp.bfloat16)
+            term = [
+                jnp.dot(combo[g], mops[g], preferred_element_type=jnp.float32).astype(
+                    jnp.bfloat16
+                )
+                for g in range(4)
+            ]
+            base[i, b] = alpha + term[0].astype(jnp.float32)
+            across[i, b] = term[2]
+            core_out[i, 0, b] = term[1]
+            core_out[i, 1, b] = term[3]
+            return carry
+
+        lax.fori_loop(0, ablk, one, 0)
+
+    def step(i, carry):
+        @pl.when(i < ranks)
+        def _():
+            compute(i)
+            core_copy(i).start()
+
+        @pl.when((i >= 1) & (i < ranks + 1))
+        def _():
+            j = i - 1
+            core_copy(j).wait_recv()
+            y_out[j] = (
+                across[j].astype(jnp.float32) + core_in[j, 1].astype(jnp.float32)
+            ).astype(jnp.bfloat16)
+            y_copy(j).start()
+
+        @pl.when(i >= 2)
+        def _():
+            j = i - 2
+            y_copy(j).wait_recv()
+            back_out[j] = (
+                base[j] + core_in[j, 0].astype(jnp.float32) + y_in[j].astype(jnp.float32)
+            ).astype(jnp.bfloat16)
+
+            @pl.when(j < ranks - 1)
+            def _():
+                back_copy(j).start()
+
+        return carry
+
+    lax.fori_loop(0, ranks + 2, step, 0)
+
+    at = block_cols(me)
+    out[:, :, at] = out[:, :, at] + back_out[ranks - 1].astype(jnp.float32)
+
+    def finish(i, carry):
+        back_copy(i).wait_recv()
+        here = block_cols(lax.rem(me + 2 * ranks - 1 - i, ranks))
+        out[:, :, here] = out[:, :, here] + back_in[i].astype(jnp.float32)
+        return carry
+
+    lax.fori_loop(0, ranks - 1, finish, 0)
+
+    def drain(i, carry):
+        core_copy(i).wait_send()
+        y_copy(i).wait_send()
+
+        @pl.when(i < ranks - 1)
+        def _():
+            back_copy(i).wait_send()
+
+        return carry
+
+    lax.fori_loop(0, ranks, drain, 0)
+
+
+def plan(ablk, send_list, mix_slot, mix_sign, mix_pair, aa_sign, aa_pair, sectors, npa):
+    ranks, _, cap = send_list.shape
+    slots = jnp.arange(ranks * cap, dtype=jnp.int32)
+    table = jnp.transpose(send_list, (1, 0, 2)).reshape(ranks, ranks * cap)
+    table = table + (slots // cap * ablk)[None, :]
+    table = jnp.repeat(table, ablk, axis=0)
+    hit = mix_slot[:, :, None] == slots[None, None, :]
+    mix_src = jnp.sum(jnp.where(hit, table[:, None, :], 0), axis=2)
+    which = jnp.arange(sectors, dtype=jnp.int32)[None, :, None]
+    sign = (1 - 2 * mix_sign)[:, None, :]
+    weight = jnp.where(mix_pair[:, None, :] == which, sign, 0).astype(jnp.float32)
+    return mix_src, weight.reshape(mix_slot.shape[0], -1), aa_sign * npa + aa_pair
+
+
+def fused(
+    ranks,
+    coeffs,
+    beta_op,
+    mix_op,
+    pair_op,
+    send_list,
+    mix_slot,
+    mix_sign,
+    mix_pair,
+    aa_src,
+    aa_sign,
+    aa_pair,
+):
+    rows_here, beta_here = coeffs.shape
+    ablk = rows_here // TILE
+    bf16, f32 = jnp.bfloat16, jnp.float32
+    sectors = mix_op.shape[1]
+    npa = pair_op.shape[0]
+    mix_src, mix_weight, aa_op = plan(
+        ablk, send_list, mix_slot, mix_sign, mix_pair, aa_sign, aa_pair, sectors, npa
+    )
+    piece = (ranks, ablk, TILE, TILE)
+    vmem, smem, anywhere = pltpu.VMEM, pltpu.SMEM, pl.ANY
+    dma = pltpu.SemaphoreType.DMA
+    result = pl.pallas_call(
+        functools.partial(kernel, ranks),
+        out_shape=jax.ShapeDtypeStruct((ablk, TILE, beta_here), f32),
+        in_specs=[pl.BlockSpec(memory_space=anywhere)] * 3
+        + [pl.BlockSpec(memory_space=vmem)]
+        + [pl.BlockSpec(memory_space=smem)] * 4,
+        out_specs=pl.BlockSpec(memory_space=vmem),
+        scratch_shapes=[
+            vmem((ranks * ablk, TILE, TILE), bf16),
+            vmem((ablk, TILE, beta_here), bf16),
+            vmem((beta_here, beta_here), bf16),
+            vmem((2 * npa, TILE, TILE), bf16),
+            vmem((sectors, TILE, TILE), bf16),
+            vmem((sectors, TILE, TILE), bf16),
+            vmem(piece, f32),
+            vmem(piece, bf16),
+            vmem((ranks, 2, ablk, TILE, TILE), bf16),
+            vmem((ranks, 2, ablk, TILE, TILE), bf16),
+            vmem(piece, bf16),
+            vmem(piece, bf16),
+            vmem(piece, bf16),
+            vmem(piece, bf16),
+            dma((4,)),
+        ]
+        + [dma((ranks,))] * 8,
+        compiler_params=pltpu.CompilerParams(
+            collective_id=0, has_side_effects=True, vmem_limit_bytes=56 * 1024 * 1024
+        ),
+        cost_estimate=pl.CostEstimate(
+            flops=6 * rows_here * beta_here * beta_here,
+            bytes_accessed=12 * rows_here * beta_here,
+            transcendentals=0,
+        ),
+    )(
+        coeffs.reshape(ablk, TILE, beta_here),
+        beta_op,
+        mix_op,
+        pair_op,
+        mix_src,
+        mix_weight,
+        aa_src,
+        aa_op,
+    )
+    return result.reshape(rows_here, beta_here)
+
+
 def solution(mesh):
+    ranks, sectors = mesh.shape["rows"], mesh.shape["sym"]
+
+    def per_device(coeffs, *rest):
+        whole_blocks = coeffs.shape[1] == ranks * TILE
+        if sectors == 4 and whole_blocks:
+            return fused(ranks, coeffs, *rest)
+        return spread(coeffs, *rest)
+
     in_specs = (
         P("rows", "sym"),
         P("sym", None, None),
         P("sym", None, None, None, None),
-        P(),
-        P(),
-        P(),
-        P(),
-        P(),
-        P(),
-        P(),
-        P(),
-    )
-    out_specs = P("rows", "sym")
+    ) + (P(),) * 8
     return jax.shard_map(
-        per_device, mesh=mesh, in_specs=in_specs, out_specs=out_specs, check_vma=False
-    )
+        per_device, mesh=mesh, in_specs=in_specs, out_specs=P("rows", "sym"), check_vma=False
+    )

time: 251 us -> 80.5 us (0.32); the launches traced: 247 us -> 79.8 us
  waiting for transfers between devices: 109 us -> 0 us
  Pallas kernels: 0 us -> 68.5 us
  local copies, waits for them, and re-layouts: 43.3 us -> 7.8 us
  matrix products: 31.6 us -> 0 us
  blocking collectives: 30.6 us -> 0 us
  between operations: 13.5 us -> 0.02 us
  starting transfers between devices: 13.4 us -> 0 us
    all_to_all x2 -> x0, waiting for transfers between devices: 109 us -> none  [the longest x1 87.2 us: per_device(): lax.all_to_all(outgoing, 'rows', split_axis=0, concat_axis=0, tiled=True)]
    pallas_call x0 -> x1, Pallas kernels: none -> 68.5 us  [fused(): pl.pallas_call(functools.partial(kernel, ranks), out_shape=jax.ShapeDtype...]
    dot_general x6 -> x0, matrix products: 31.6 us -> none  [the longest x1 12 us: per_device(): jnp.einsum('cpki,pkg->cpgi', picked, aa_weight, preferred_element_type=jn...]
    all_to_all x1 -> x0, blocking collectives: 30.6 us -> none  [per_device(): lax.all_to_all(alpha_part.astype(jnp.bfloat16), 'rows', split_axis=1, con...]
    gather x3 -> x0, local copies, waits for them, and re-layouts: 14.6 us -> none  [the longest x1 8.63 us: per_device(): picked = jnp.take(col_blocks, aa_src, axis=1)]
    all_to_all x2 -> x0, starting transfers between devices: 13.4 us -> none  [the longest x1 7.02 us: per_device(): lax.all_to_all(flipped, 'rows', split_axis=0, concat_axis=1, tiled=True)]
    convert_element_type x2 -> x0, local copies, waits for them, and re-layouts: 7.52 us -> none  [the longest x1 7.52 us: per_device(): products.reshape(row_count, beta_here).astype(jnp.bfloat16)]
    reshape x2 -> x0, local copies, waits for them, and re-layouts: 6.44 us -> none  [the longest x1 4.83 us: per_device(): inputs = inputs.reshape(sectors, rows_here, BT, TILE)]
  transfers between devices with their start and end apart: 3 -> 0, of which waited for: 2 -> 0; matrix products, arithmetic and copies ran while one was open for 14% -> 0% of each run, Pallas kernels for 0% -> 0%
where the time goes in v1:
time: 80.5 us; the launch traced here: 79.8 us
  Pallas kernels  68.5 us (85%)
  local copies, waits for them, and re-layouts  7.8 us (10%)
  other arithmetic  3.43 us (4%)
    pallas_call x1, Pallas kernels, fused(): pl.pallas_call(functools.partial(kernel, ranks), out_shape=jax.ShapeDtype...  68.5 us
    unnamed x4, local copies, waits for them, and re-layouts  6.04 us

profile of v1, /device:TPU:10, one launch (start us, length us, event | category | flops | bytes accessed | tf_op | source)
XLA Modules:
  0.0 79.8 jit_solution(8287502806503869571)
XLA Ops:
  0.0 0.1 eq.39
  0.1 0.8 broadcast_add_fusion
  0.9 0.1 copy.40
  0.9 0.7 multiply_subtract_fusion
  1.6 0.1 copy.41
  1.7 0.7 select_reduce_fusion
  2.5 0.7 copy.47.mix_src
  3.1 1.4 %copy.48.aa_src = s32[32,8]{1,0:T(8,128)} copy(s32[32,8]{0,1:T(8,128)} %param.19) | data formatting | bytes 2048 | tf_op args[8]
  4.5 0.8 copy.44
  5.3 0.8 copy.46
  6.0 0.6 multiply_add_fusion.aa_op
  6.6 0.1 copy.43
  6.7 0.7 eq.36
  7.4 0.1 copy.42
  7.5 0.6 select_convert_fusion.mix_weight
  8.1 68.5 %shard_map.109 = f32[4,128,1024]{2,1,0:T(8,128)} custom-call(bf16[4,128,1024]{2,1,0:T(8,128)(2,1)} %bitcast.13, bf16[1,1024,1024]{2,1,0:T(8,128)(2,1)} %beta_op.1, bf16[1,4,8,128,128]{4,3,2,1,0:T(8,128)(2,1)} %mix_op.1, bf16[8,128,128]{2,1,0:T(8,128)(2,1)} %pair_op.1, s32[32,16]{1,0:T(8,128)} %copy.47.mix_src, f32[32,64]{1,0:T(8,128)} %select_convert_fusion.mix_weight, ...), custom_call_target="tpu_custom_call" | custom-call | flops 3221225472 | bytes 6291456 | tf_op jit(solution)/shard_map/pallas_call | solution.py:374
  76.6 3.2 %copy.50 = f32[512,1024]{1,0:T(8,128)} copy(f32[512,1024]{1,0:T(8,128)} %bitcast.8) | data formatting | bytes 4194304
  (4 shorter events, 0.0 us)

commit v2 on v1

--- a/solution.py
+++ b/solution.py
@@ -101,17 +101,20 @@
     beta_op,
     mix_op,
     pair_op,
-    mix_src,
-    mix_weight,
+    send_list,
+    mix_slot,
+    mix_sign,
+    mix_pair,
     aa_src,
-    aa_op,
+    aa_sign,
+    aa_pair,
     out,
     cols,
     mine,
     beta,
-    pairs,
     mops,
-    combo,
+    alphas,
+    mixes,
     base,
     across,
     core_out,
@@ -131,9 +134,10 @@
     back_recv,
 ):
     ablk, _, beta_here = coeffs.shape
-    entries = mix_src.shape[1]
-    ka = aa_src.shape[1]
+    entries = mix_slot.shape[0]
+    ka = aa_src.shape[0]
     npa = pair_op.shape[0]
+    sectors = mops.shape[0]
     me = lax.axis_index("rows")
     sym = lax.axis_index("sym")
     core_mate = sym + 1 - 2 * lax.rem(sym, 2)
@@ -190,10 +194,6 @@
     for i in range(ranks - 1):
         go(i).start()
 
-    for k in range(npa):
-        pairs[k] = pair_op[k]
-        pairs[npa + k] = -pair_op[k]
-
     load_mine.wait()
     load_beta.wait()
     width = 2 * TILE
@@ -208,9 +208,31 @@
             )
 
     load_mops.wait()
+
+    def products(r):
+        stacked = pair_op[...].reshape(npa * TILE, TILE)
+
+        def one(b, carry):
+            block = r * ablk + b
+            x = cols[block]
+            alphas[block] = jnp.dot(
+                stacked, x, preferred_element_type=jnp.float32
+            ).reshape(npa, TILE, TILE)
+            for g in range(sectors):
+                mixes[block, g] = jnp.dot(x, mops[g], preferred_element_type=jnp.float32)
+            return carry
+
+        lax.fori_loop(0, ablk, one, 0)
+
     load_own.wait()
-    for i in range(ranks - 1):
+    products(me)
+
+    def arrive(i, carry):
         go_in(i).wait_recv()
+        products(lax.rem(me + 2 * ranks - 1 - i, ranks))
+        return carry
+
+    lax.fori_loop(0, ranks - 1, arrive, 0)
     for i in range(ranks - 1):
         go(i).wait_send()
 
@@ -249,30 +271,33 @@
 
         def one(b, carry):
             p = r * ablk + b
-            alpha = jnp.dot(
-                jnp.concatenate([pairs[aa_op[p, k]] for k in range(ka)], axis=1),
-                jnp.concatenate([cols[aa_src[p, k]] for k in range(ka)], axis=0),
-                preferred_element_type=jnp.float32,
-            )
-            sources = [mix_src[p, l] for l in range(entries)]
+            picks, signs = [], []
+            for k in range(ka):
+                picks.append((aa_src[k, p], aa_pair[k, p]))
+                signs.append((1 - 2 * aa_sign[k, p]).astype(jnp.float32))
+            finds, weights = [], []
+            for l in range(entries):
+                slot = mix_slot[l, p]
+                s = lax.div(slot, CAP)
+                pair = mix_pair[l, p]
+                sign = (1 - 2 * mix_sign[l, p]).astype(jnp.float32)
+                finds.append((s * ablk + send_list[s, slot - s * CAP, r], pair))
+                weights.append([jnp.where(pair == g, sign, 0.0) for g in range(sectors)])
             for c in range(TILE // CHUNK):
-                total = [jnp.zeros((CHUNK, TILE), jnp.float32) for _ in range(4)]
+                at = slice(c * CHUNK, (c + 1) * CHUNK)
+                total = [jnp.zeros((CHUNK, TILE), jnp.float32) for _ in range(sectors)]
                 for l in range(entries):
-                    x = cols[sources[l], c * CHUNK : (c + 1) * CHUNK, :].astype(jnp.float32)
-                    for g in range(4):
-                        total[g] = total[g] + mix_weight[p, g * entries + l] * x
-                for g in range(4):
-                    combo[g, c * CHUNK : (c + 1) * CHUNK, :] = total[g].astype(jnp.bfloat16)
-            term = [
-                jnp.dot(combo[g], mops[g], preferred_element_type=jnp.float32).astype(
-                    jnp.bfloat16
-                )
-                for g in range(4)
-            ]
-            base[i, b] = alpha + term[0].astype(jnp.float32)
-            across[i, b] = term[2]
-            core_out[i, 0, b] = term[1]
-            core_out[i, 1, b] = term[3]
+                    x = mixes[finds[l][0], finds[l][1], at, :]
+                    for g in range(sectors):
+                        total[g] = total[g] + weights[l][g] * x
+                term = [t.astype(jnp.bfloat16) for t in total]
+                across[i, b, at, :] = term[2]
+                core_out[i, 0, b, at, :] = term[1]
+                core_out[i, 1, b, at, :] = term[3]
+                alpha = term[0].astype(jnp.float32)
+                for k in range(ka):
+                    alpha = alpha + signs[k] * alphas[picks[k][0], picks[k][1], at, :]
+                base[i, b, at, :] = alpha
             return carry
 
         lax.fori_loop(0, ablk, one, 0)
@@ -330,20 +355,6 @@
         return carry
 
     lax.fori_loop(0, ranks, drain, 0)
-
-
-def plan(ablk, send_list, mix_slot, mix_sign, mix_pair, aa_sign, aa_pair, sectors, npa):
-    ranks, _, cap = send_list.shape
-    slots = jnp.arange(ranks * cap, dtype=jnp.int32)
-    table = jnp.transpose(send_list, (1, 0, 2)).reshape(ranks, ranks * cap)
-    table = table + (slots // cap * ablk)[None, :]
-    table = jnp.repeat(table, ablk, axis=0)
-    hit = mix_slot[:, :, None] == slots[None, None, :]
-    mix_src = jnp.sum(jnp.where(hit, table[:, None, :], 0), axis=2)
-    which = jnp.arange(sectors, dtype=jnp.int32)[None, :, None]
-    sign = (1 - 2 * mix_sign)[:, None, :]
-    weight = jnp.where(mix_pair[:, None, :] == which, sign, 0).astype(jnp.float32)
-    return mix_src, weight.reshape(mix_slot.shape[0], -1), aa_sign * npa + aa_pair
 
 
 def fused(
@@ -365,9 +376,6 @@
     bf16, f32 = jnp.bfloat16, jnp.float32
     sectors = mix_op.shape[1]
     npa = pair_op.shape[0]
-    mix_src, mix_weight, aa_op = plan(
-        ablk, send_list, mix_slot, mix_sign, mix_pair, aa_sign, aa_pair, sectors, npa
-    )
     piece = (ranks, ablk, TILE, TILE)
     vmem, smem, anywhere = pltpu.VMEM, pltpu.SMEM, pl.ANY
     dma = pltpu.SemaphoreType.DMA
@@ -376,15 +384,15 @@
         out_shape=jax.ShapeDtypeStruct((ablk, TILE, beta_here), f32),
         in_specs=[pl.BlockSpec(memory_space=anywhere)] * 3
         + [pl.BlockSpec(memory_space=vmem)]
-        + [pl.BlockSpec(memory_space=smem)] * 4,
+        + [pl.BlockSpec(memory_space=smem)] * 7,
         out_specs=pl.BlockSpec(memory_space=vmem),
         scratch_shapes=[
             vmem((ranks * ablk, TILE, TILE), bf16),
             vmem((ablk, TILE, beta_here), bf16),
             vmem((beta_here, beta_here), bf16),
-            vmem((2 * npa, TILE, TILE), bf16),
             vmem((sectors, TILE, TILE), bf16),
-            vmem((sectors, TILE, TILE), bf16),
+            vmem((ranks * ablk, npa, TILE, TILE), f32),
+            vmem((ranks * ablk, sectors, TILE, TILE), f32),
             vmem(piece, f32),
             vmem(piece, bf16),
             vmem((ranks, 2, ablk, TILE, TILE), bf16),
@@ -409,10 +417,13 @@
         beta_op,
         mix_op,
         pair_op,
-        mix_src,
-        mix_weight,
-        aa_src,
-        aa_op,
+        jnp.transpose(send_list, (0, 2, 1)),
+        mix_slot.T,
+        mix_sign.T,
+        mix_pair.T,
+        aa_src.T,
+        aa_sign.T,
+        aa_pair.T,
     )
     return result.reshape(rows_here, beta_here)
 

time: 80.5 us -> 74.4 us (0.924)
  local copies, waits for them, and re-layouts: 7.8 us -> 3.16 us
  other arithmetic: 3.43 us -> 0 us
  Pallas kernels: 68.5 us -> 71 us
    unnamed x4 -> x1, local copies, waits for them, and re-layouts: 6.04 us -> 3.16 us
    pallas_call x1, Pallas kernels: 68.5 us -> 71 us  [fused(): pl.pallas_call(functools.partial(kernel, ranks), out_shape=jax.ShapeDtype...]
    add x2 -> x0, other arithmetic: 1.37 us -> none  [the longest x1 0.77 us: plan(): table = table + (slots // cap * ablk)[None, :]]
    eq x4 -> x0, local copies, waits for them, and re-layouts: 0.87 us -> none  [plan(): mix_pair[:, None, :] == which]
where the time goes in v2:
time: 74.4 us; the launch traced here: 74.2 us
  Pallas kernels  71 us (95%)
  local copies, waits for them, and re-layouts  3.16 us (4%)
    pallas_call x1, Pallas kernels, fused(): pl.pallas_call(functools.partial(kernel, ranks), out_shape=jax.ShapeDtype...  71 us
    unnamed x1, local copies, waits for them, and re-layouts  3.16 us

profile of v2, /device:TPU:10, one launch (start us, length us, event | category | flops | bytes accessed | tf_op | source)
XLA Modules:
  0.0 74.2 jit_solution(7110805611972629352)
XLA Ops:
  0.0 71.0 %shard_map.109 = f32[4,128,1024]{2,1,0:T(8,128)} custom-call(bf16[4,128,1024]{2,1,0:T(8,128)(2,1)} %bitcast.10, bf16[1,1024,1024]{2,1,0:T(8,128)(2,1)} %beta_op.1, bf16[1,4,8,128,128]{4,3,2,1,0:T(8,128)(2,1)} %mix_op.1, bf16[8,128,128]{2,1,0:T(8,128)(2,1)} %pair_op.1, s32[8,2,8]{2,1,0:T(2,128)} %bitcast.11, s32[16,32]{1,0:T(8,128)} %bitcast.12, ...), custom_call_target="tpu_custom_call" | custom-call | flops 3221225472 | bytes 6291456 | tf_op jit(solution)/shard_map/pallas_call | solution.py:382
  71.0 3.2 %copy.13 = f32[512,1024]{1,0:T(8,128)} copy(f32[512,1024]{1,0:T(8,128)} %bitcast.9) | data formatting | bytes 4194304

commit v3 on v2

--- a/solution.py
+++ b/solution.py
@@ -115,21 +115,19 @@
     mops,
     alphas,
     mixes,
-    base,
-    across,
-    core_out,
-    core_in,
-    y_out,
-    y_in,
     back_out,
     back_in,
     local_sem,
     go_send,
     go_recv,
-    core_send,
-    core_recv,
+    op_send,
+    op_recv,
     y_send,
     y_recv,
+    near_send,
+    near_recv,
+    far_send,
+    far_recv,
     back_send,
     back_recv,
 ):
@@ -142,6 +140,8 @@
     sym = lax.axis_index("sym")
     core_mate = sym + 1 - 2 * lax.rem(sym, 2)
     y_mate = lax.rem(sym + 2, 4)
+    far_mate = y_mate + 1 - 2 * lax.rem(y_mate, 2)
+    mates = (sym, core_mate, y_mate, far_mate)
 
     def block_cols(r):
         return pl.ds(pl.multiple_of(r * TILE, TILE), TILE)
@@ -151,9 +151,9 @@
 
     load_mine = pltpu.make_async_copy(coeffs, mine, local_sem.at[0])
     load_beta = pltpu.make_async_copy(beta_op.at[0], beta, local_sem.at[1])
-    load_mops = pltpu.make_async_copy(mix_op.at[0, :, me], mops, local_sem.at[2])
+    load_mops = pltpu.make_async_copy(mix_op.at[0, 0, me], mops.at[0], local_sem.at[2])
     load_own = pltpu.make_async_copy(
-        coeffs.at[:, :, block_cols(me)], cols.at[blocks_of(me)], local_sem.at[3]
+        coeffs.at[:, :, block_cols(me)], cols.at[0, blocks_of(me)], local_sem.at[3]
     )
     load_mine.start()
     load_beta.start()
@@ -165,15 +165,15 @@
         pl.semaphore_signal(
             barrier, inc=1, device_id={"rows": lax.rem(me + i, ranks)}, device_id_type=MESH
         )
-    pl.semaphore_signal(barrier, inc=1, device_id={"sym": core_mate}, device_id_type=MESH)
-    pl.semaphore_signal(barrier, inc=1, device_id={"sym": y_mate}, device_id_type=MESH)
-    pl.semaphore_wait(barrier, ranks + 1)
+    for g in range(1, sectors):
+        pl.semaphore_signal(barrier, inc=1, device_id={"sym": mates[g]}, device_id_type=MESH)
+    pl.semaphore_wait(barrier, ranks + sectors - 2)
 
     def go(i):
         r = lax.rem(me + 1 + i, ranks)
         return pltpu.make_async_remote_copy(
             src_ref=coeffs.at[:, :, block_cols(r)],
-            dst_ref=cols.at[blocks_of(me)],
+            dst_ref=cols.at[0, blocks_of(me)],
             send_sem=go_send.at[i],
             recv_sem=go_recv.at[i],
             device_id={"rows": r},
@@ -184,15 +184,50 @@
         r = lax.rem(me + 2 * ranks - 1 - i, ranks)
         return pltpu.make_async_remote_copy(
             src_ref=coeffs.at[:, :, block_cols(r)],
-            dst_ref=cols.at[blocks_of(r)],
+            dst_ref=cols.at[0, blocks_of(r)],
             send_sem=go_send.at[i],
             recv_sem=go_recv.at[i],
             device_id={"rows": r},
             device_id_type=MESH,
         )
 
+    def op_copy(g):
+        return pltpu.make_async_remote_copy(
+            src_ref=mix_op.at[0, g, me],
+            dst_ref=mops.at[g],
+            send_sem=op_send.at[g],
+            recv_sem=op_recv.at[g],
+            device_id={"sym": mates[g]},
+            device_id_type=MESH,
+        )
+
+    def forward(j, source, target, mate, send_sem, recv_sem):
+        part = blocks_of(lax.rem(me + ranks - j, ranks))
+        return pltpu.make_async_remote_copy(
+            src_ref=cols.at[source, part],
+            dst_ref=cols.at[target, part],
+            send_sem=send_sem.at[j],
+            recv_sem=recv_sem.at[j],
+            device_id={"sym": mate},
+            device_id_type=MESH,
+        )
+
+    def y_copy(j):
+        return forward(j, 0, 2, y_mate, y_send, y_recv)
+
+    def near_copy(j):
+        return forward(j, 0, 1, core_mate, near_send, near_recv)
+
+    def far_copy(j):
+        return forward(j, 2, 3, core_mate, far_send, far_recv)
+
     for i in range(ranks - 1):
         go(i).start()
+    load_own.wait()
+    y_copy(0).start()
+    near_copy(0).start()
+    for g in range(1, sectors):
+        op_copy(g).start()
 
     load_mine.wait()
     load_beta.wait()
@@ -208,53 +243,56 @@
             )
 
     load_mops.wait()
-
-    def products(r):
+    for g in range(1, sectors):
+        op_copy(g).wait_recv()
+
+    def times_pairs(j):
         stacked = pair_op[...].reshape(npa * TILE, TILE)
 
         def one(b, carry):
-            block = r * ablk + b
-            x = cols[block]
+            block = lax.rem(me + ranks - j, ranks) * ablk + b
             alphas[block] = jnp.dot(
-                stacked, x, preferred_element_type=jnp.float32
+                stacked, cols[0, block], preferred_element_type=jnp.float32
             ).reshape(npa, TILE, TILE)
-            for g in range(sectors):
-                mixes[block, g] = jnp.dot(x, mops[g], preferred_element_type=jnp.float32)
             return carry
 
         lax.fori_loop(0, ablk, one, 0)
 
-    load_own.wait()
-    products(me)
-
-    def arrive(i, carry):
-        go_in(i).wait_recv()
-        products(lax.rem(me + 2 * ranks - 1 - i, ranks))
+    def times_mix(j, g):
+        part = blocks_of(lax.rem(me + ranks - j, ranks))
+        x = cols[g, part].reshape(ablk * TILE, TILE)
+        mixes[g, part] = jnp.dot(x, mops[g], preferred_element_type=jnp.float32).reshape(
+            ablk, TILE, TILE
+        )
+
+    def arrive(j, carry):
+        @pl.when((j >= 1) & (j < ranks))
+        def _():
+            go_in(j - 1).wait_recv()
+            y_copy(j).start()
+            near_copy(j).start()
+
+        @pl.when(j < ranks)
+        def _():
+            times_pairs(j)
+            times_mix(j, 0)
+
+        @pl.when((j >= 1) & (j < ranks + 1))
+        def _():
+            y_copy(j - 1).wait_recv()
+            far_copy(j - 1).start()
+            near_copy(j - 1).wait_recv()
+            times_mix(j - 1, 1)
+            times_mix(j - 1, 2)
+
+        @pl.when(j >= 2)
+        def _():
+            far_copy(j - 2).wait_recv()
+            times_mix(j - 2, 3)
+
         return carry
 
-    lax.fori_loop(0, ranks - 1, arrive, 0)
-    for i in range(ranks - 1):
-        go(i).wait_send()
-
-    def core_copy(i):
-        return pltpu.make_async_remote_copy(
-            src_ref=core_out.at[i],
-            dst_ref=core_in.at[i],
-            send_sem=core_send.at[i],
-            recv_sem=core_recv.at[i],
-            device_id={"sym": core_mate},
-            device_id_type=MESH,
-        )
-
-    def y_copy(i):
-        return pltpu.make_async_remote_copy(
-            src_ref=y_out.at[i],
-            dst_ref=y_in.at[i],
-            send_sem=y_send.at[i],
-            recv_sem=y_recv.at[i],
-            device_id={"sym": y_mate},
-            device_id_type=MESH,
-        )
+    lax.fori_loop(0, ranks + 2, arrive, 0)
 
     def back_copy(i):
         return pltpu.make_async_remote_copy(
@@ -271,67 +309,37 @@
 
         def one(b, carry):
             p = r * ablk + b
-            picks, signs = [], []
+            picks, signs, finds, flips = [], [], [], []
             for k in range(ka):
                 picks.append((aa_src[k, p], aa_pair[k, p]))
                 signs.append((1 - 2 * aa_sign[k, p]).astype(jnp.float32))
-            finds, weights = [], []
             for l in range(entries):
                 slot = mix_slot[l, p]
                 s = lax.div(slot, CAP)
-                pair = mix_pair[l, p]
-                sign = (1 - 2 * mix_sign[l, p]).astype(jnp.float32)
-                finds.append((s * ablk + send_list[s, slot - s * CAP, r], pair))
-                weights.append([jnp.where(pair == g, sign, 0.0) for g in range(sectors)])
+                finds.append((mix_pair[l, p], s * ablk + send_list[s, slot - s * CAP, r]))
+                flips.append((1 - 2 * mix_sign[l, p]).astype(jnp.float32))
             for c in range(TILE // CHUNK):
                 at = slice(c * CHUNK, (c + 1) * CHUNK)
-                total = [jnp.zeros((CHUNK, TILE), jnp.float32) for _ in range(sectors)]
+                total = jnp.zeros((CHUNK, TILE), jnp.float32)
+                for k in range(ka):
+                    total = total + signs[k] * alphas[picks[k][0], picks[k][1], at, :]
                 for l in range(entries):
-                    x = mixes[finds[l][0], finds[l][1], at, :]
-                    for g in range(sectors):
-                        total[g] = total[g] + weights[l][g] * x
-                term = [t.astype(jnp.bfloat16) for t in total]
-                across[i, b, at, :] = term[2]
-                core_out[i, 0, b, at, :] = term[1]
-                core_out[i, 1, b, at, :] = term[3]
-                alpha = term[0].astype(jnp.float32)
-                for k in range(ka):
-                    alpha = alpha + signs[k] * alphas[picks[k][0], picks[k][1], at, :]
-                base[i, b, at, :] = alpha
+                    total = total + flips[l] * mixes[finds[l][0], finds[l][1], at, :]
+                back_out[i, b, at, :] = total.astype(jnp.bfloat16)
             return carry
 
         lax.fori_loop(0, ablk, one, 0)
 
     def step(i, carry):
-        @pl.when(i < ranks)
-        def _():
-            compute(i)
-            core_copy(i).start()
-
-        @pl.when((i >= 1) & (i < ranks + 1))
-        def _():
-            j = i - 1
-            core_copy(j).wait_recv()
-            y_out[j] = (
-                across[j].astype(jnp.float32) + core_in[j, 1].astype(jnp.float32)
-            ).astype(jnp.bfloat16)
-            y_copy(j).start()
-
-        @pl.when(i >= 2)
-        def _():
-            j = i - 2
-            y_copy(j).wait_recv()
-            back_out[j] = (
-                base[j] + core_in[j, 0].astype(jnp.float32) + y_in[j].astype(jnp.float32)
-            ).astype(jnp.bfloat16)
-
-            @pl.when(j < ranks - 1)
-            def _():
-                back_copy(j).start()
+        compute(i)
+
+        @pl.when(i < ranks - 1)
+        def _():
+            back_copy(i).start()
 
         return carry
 
-    lax.fori_loop(0, ranks + 2, step, 0)
+    lax.fori_loop(0, ranks, step, 0)
 
     at = block_cols(me)
     out[:, :, at] = out[:, :, at] + back_out[ranks - 1].astype(jnp.float32)
@@ -345,16 +353,20 @@
     lax.fori_loop(0, ranks - 1, finish, 0)
 
     def drain(i, carry):
-        core_copy(i).wait_send()
         y_copy(i).wait_send()
+        near_copy(i).wait_send()
+        far_copy(i).wait_send()
 
         @pl.when(i < ranks - 1)
         def _():
+            go(i).wait_send()
             back_copy(i).wait_send()
 
         return carry
 
     lax.fori_loop(0, ranks, drain, 0)
+    for g in range(1, sectors):
+        op_copy(g).wait_send()
 
 
 def fused(
@@ -387,21 +399,19 @@
         + [pl.BlockSpec(memory_space=smem)] * 7,
         out_specs=pl.BlockSpec(memory_space=vmem),
         scratch_shapes=[
-            vmem((ranks * ablk, TILE, TILE), bf16),
+            vmem((sectors, ranks * ablk, TILE, TILE), bf16),
             vmem((ablk, TILE, beta_here), bf16),
             vmem((beta_here, beta_here), bf16),
             vmem((sectors, TILE, TILE), bf16),
             vmem((ranks * ablk, npa, TILE, TILE), f32),
-            vmem((ranks * ablk, sectors, TILE, TILE), f32),
-            vmem(piece, f32),
-            vmem(piece, bf16),
-            vmem((ranks, 2, ablk, TILE, TILE), bf16),
-            vmem((ranks, 2, ablk, TILE, TILE), bf16),
-            vmem(piece, bf16),
-            vmem(piece, bf16),
+            vmem((sectors, ranks * ablk, TILE, TILE), f32),
             vmem(piece, bf16),
             vmem(piece, bf16),
             dma((4,)),
+            dma((ranks,)),
+            dma((ranks,)),
+            dma((sectors,)),
+            dma((sectors,)),
         ]
         + [dma((ranks,))] * 8,
         compiler_params=pltpu.CompilerParams(

time: 74.4 us -> 74.7 us (level)
  no operation moved by 1% of the time
where the time goes in v3:
time: 74.7 us; the launch traced here: 74.2 us
  Pallas kernels  71 us (95%)
  local copies, waits for them, and re-layouts  3.16 us (4%)
    pallas_call x1, Pallas kernels, fused(): pl.pallas_call(functools.partial(kernel, ranks), out_shape=jax.ShapeDtype...  71 us
    unnamed x1, local copies, waits for them, and re-layouts  3.16 us

profile of v3, /device:TPU:10, one launch (start us, length us, event | category | flops | bytes accessed | tf_op | source)
XLA Modules:
  0.0 74.2 jit_solution(18373047455454381935)
XLA Ops:
  0.0 71.0 %shard_map.109 = f32[4,128,1024]{2,1,0:T(8,128)} custom-call(bf16[4,128,1024]{2,1,0:T(8,128)(2,1)} %bitcast.10, bf16[1,1024,1024]{2,1,0:T(8,128)(2,1)} %beta_op.1, bf16[1,4,8,128,128]{4,3,2,1,0:T(8,128)(2,1)} %mix_op.1, bf16[8,128,128]{2,1,0:T(8,128)(2,1)} %pair_op.1, s32[8,2,8]{2,1,0:T(2,128)} %bitcast.11, s32[16,32]{1,0:T(8,128)} %bitcast.12, ...), custom_call_target="tpu_custom_call" | custom-call | flops 3221225472 | bytes 6291456 | tf_op jit(solution)/shard_map/pallas_call | solution.py:394
  71.0 3.2 %copy.13 = f32[512,1024]{1,0:T(8,128)} copy(f32[512,1024]{1,0:T(8,128)} %bitcast.9) | data formatting | bytes 4194304

commit v4 on v3

--- a/solution.py
+++ b/solution.py
@@ -108,6 +108,8 @@
     aa_src,
     aa_sign,
     aa_pair,
+    local,
+    back,
     out,
     cols,
     mine,
@@ -116,7 +118,6 @@
     alphas,
     mixes,
     back_out,
-    back_in,
     local_sem,
     go_send,
     go_recv,
@@ -143,6 +144,18 @@
     far_mate = y_mate + 1 - 2 * lax.rem(y_mate, 2)
     mates = (sym, core_mate, y_mate, far_mate)
 
+    def shift(i):
+        return ranks // 2 + lax.div(i + 1, 2) * (2 * lax.rem(i, 2) - 1)
+
+    def target(i):
+        return lax.rem(me + shift(i), ranks)
+
+    def origin(i):
+        return lax.rem(me + ranks - shift(i), ranks)
+
+    def held(j):
+        return origin(lax.rem(j + ranks - 1, ranks))
+
     def block_cols(r):
         return pl.ds(pl.multiple_of(r * TILE, TILE), TILE)
 
@@ -170,7 +183,7 @@
     pl.semaphore_wait(barrier, ranks + sectors - 2)
 
     def go(i):
-        r = lax.rem(me + 1 + i, ranks)
+        r = target(i)
         return pltpu.make_async_remote_copy(
             src_ref=coeffs.at[:, :, block_cols(r)],
             dst_ref=cols.at[0, blocks_of(me)],
@@ -181,7 +194,7 @@
         )
 
     def go_in(i):
-        r = lax.rem(me + 2 * ranks - 1 - i, ranks)
+        r = origin(i)
         return pltpu.make_async_remote_copy(
             src_ref=coeffs.at[:, :, block_cols(r)],
             dst_ref=cols.at[0, blocks_of(r)],
@@ -201,11 +214,11 @@
             device_id_type=MESH,
         )
 
-    def forward(j, source, target, mate, send_sem, recv_sem):
-        part = blocks_of(lax.rem(me + ranks - j, ranks))
+    def forward(j, source, goal, mate, send_sem, recv_sem):
+        part = blocks_of(held(j))
         return pltpu.make_async_remote_copy(
             src_ref=cols.at[source, part],
-            dst_ref=cols.at[target, part],
+            dst_ref=cols.at[goal, part],
             send_sem=send_sem.at[j],
             recv_sem=recv_sem.at[j],
             device_id={"sym": mate},
@@ -242,6 +255,8 @@
                 mine[m], beta[:, at], preferred_element_type=jnp.float32
             )
 
+    save = pltpu.make_async_copy(out, local, local_sem.at[0])
+    save.start()
     load_mops.wait()
     for g in range(1, sectors):
         op_copy(g).wait_recv()
@@ -250,7 +265,7 @@
         stacked = pair_op[...].reshape(npa * TILE, TILE)
 
         def one(b, carry):
-            block = lax.rem(me + ranks - j, ranks) * ablk + b
+            block = held(j) * ablk + b
             alphas[block] = jnp.dot(
                 stacked, cols[0, block], preferred_element_type=jnp.float32
             ).reshape(npa, TILE, TILE)
@@ -259,7 +274,7 @@
         lax.fori_loop(0, ablk, one, 0)
 
     def times_mix(j, g):
-        part = blocks_of(lax.rem(me + ranks - j, ranks))
+        part = blocks_of(held(j))
         x = cols[g, part].reshape(ablk * TILE, TILE)
         mixes[g, part] = jnp.dot(x, mops[g], preferred_element_type=jnp.float32).reshape(
             ablk, TILE, TILE
@@ -297,15 +312,25 @@
     def back_copy(i):
         return pltpu.make_async_remote_copy(
             src_ref=back_out.at[i],
-            dst_ref=back_in.at[i],
+            dst_ref=back.at[me],
             send_sem=back_send.at[i],
             recv_sem=back_recv.at[i],
-            device_id={"rows": lax.rem(me + 1 + i, ranks)},
+            device_id={"rows": target(i)},
             device_id_type=MESH,
         )
 
+    def back_arrival(i):
+        return pltpu.make_async_remote_copy(
+            src_ref=back_out.at[i],
+            dst_ref=back.at[origin(i)],
+            send_sem=back_send.at[i],
+            recv_sem=back_recv.at[i],
+            device_id={"rows": origin(i)},
+            device_id_type=MESH,
+        )
+
     def compute(i):
-        r = lax.rem(me + 1 + i, ranks)
+        r = target(i)
 
         def one(b, carry):
             p = r * ablk + b
@@ -341,16 +366,16 @@
 
     lax.fori_loop(0, ranks, step, 0)
 
-    at = block_cols(me)
-    out[:, :, at] = out[:, :, at] + back_out[ranks - 1].astype(jnp.float32)
+    keep_own = pltpu.make_async_copy(back_out.at[ranks - 1], back.at[me], local_sem.at[3])
+    keep_own.start()
 
     def finish(i, carry):
-        back_copy(i).wait_recv()
-        here = block_cols(lax.rem(me + 2 * ranks - 1 - i, ranks))
-        out[:, :, here] = out[:, :, here] + back_in[i].astype(jnp.float32)
+        back_arrival(i).wait_recv()
         return carry
 
     lax.fori_loop(0, ranks - 1, finish, 0)
+    keep_own.wait()
+    save.wait()
 
     def drain(i, carry):
         y_copy(i).wait_send()
@@ -367,6 +392,12 @@
     lax.fori_loop(0, ranks, drain, 0)
     for g in range(1, sectors):
         op_copy(g).wait_send()
+
+
+def add(local, back, out):
+    for t in range(back.shape[0]):
+        at = slice(t * TILE, (t + 1) * TILE)
+        out[0, :, at] = local[0, :, at] + back[t, 0].astype(jnp.float32)
 
 
 def fused(
@@ -391,21 +422,24 @@
     piece = (ranks, ablk, TILE, TILE)
     vmem, smem, anywhere = pltpu.VMEM, pltpu.SMEM, pl.ANY
     dma = pltpu.SemaphoreType.DMA
-    result = pl.pallas_call(
+    local, back = pl.pallas_call(
         functools.partial(kernel, ranks),
-        out_shape=jax.ShapeDtypeStruct((ablk, TILE, beta_here), f32),
+        out_shape=(
+            jax.ShapeDtypeStruct((ablk, TILE, beta_here), f32),
+            jax.ShapeDtypeStruct(piece, bf16),
+        ),
         in_specs=[pl.BlockSpec(memory_space=anywhere)] * 3
         + [pl.BlockSpec(memory_space=vmem)]
         + [pl.BlockSpec(memory_space=smem)] * 7,
-        out_specs=pl.BlockSpec(memory_space=vmem),
+        out_specs=(pl.BlockSpec(memory_space=anywhere),) * 2,
         scratch_shapes=[
+            vmem((ablk, TILE, beta_here), f32),
             vmem((sectors, ranks * ablk, TILE, TILE), bf16),
             vmem((ablk, TILE, beta_here), bf16),
             vmem((beta_here, beta_here), bf16),
             vmem((sectors, TILE, TILE), bf16),
             vmem((ranks * ablk, npa, TILE, TILE), f32),
             vmem((sectors, ranks * ablk, TILE, TILE), f32),
-            vmem(piece, bf16),
             vmem(piece, bf16),
             dma((4,)),
             dma((ranks,)),
@@ -435,6 +469,16 @@
         aa_sign.T,
         aa_pair.T,
     )
+    result = pl.pallas_call(
+        add,
+        grid=(ablk,),
+        out_shape=jax.ShapeDtypeStruct((ablk, TILE, beta_here), f32),
+        in_specs=[
+            pl.BlockSpec((1, TILE, beta_here), lambda b: (b, 0, 0)),
+            pl.BlockSpec((ranks, 1, TILE, TILE), lambda b: (0, b, 0, 0)),
+        ],
+        out_specs=pl.BlockSpec((1, TILE, beta_here), lambda b: (b, 0, 0)),
+    )(local, back)
     return result.reshape(rows_here, beta_here)
 
 
@@ -443,7 +487,7 @@
 
     def per_device(coeffs, *rest):
         whole_blocks = coeffs.shape[1] == ranks * TILE
-        if sectors == 4 and whole_blocks:
+        if sectors == 4 and ranks % 2 == 0 and whole_blocks:
             return fused(ranks, coeffs, *rest)
         return spread(coeffs, *rest)
 

time: 74.7 us -> 74.3 us (level)
  local copies, waits for them, and re-layouts: 3.16 us -> 0 us
  Pallas kernels: 71 us -> 73.5 us
    unnamed x1 -> x0, local copies, waits for them, and re-layouts: 3.16 us -> none
    pallas_call x1 -> x2, Pallas kernels: 71 us -> 73.5 us  [the longest x1 69.5 us: fused(): pl.pallas_call(functools.partial(kernel, ranks), out_shape=(jax.ShapeDtyp...]
where the time goes in v4:
time: 74.3 us; the launch traced here: 73.5 us
  Pallas kernels  73.5 us (99%)
    pallas_call x1, Pallas kernels, fused(): pl.pallas_call(functools.partial(kernel, ranks), out_shape=(jax.ShapeDtyp...  69.5 us
    pallas_call x1, Pallas kernels, fused(): pl.pallas_call(add, grid=(ablk,), out_shape=jax.ShapeDtypeStruct((ablk, T...  4 us

profile of v4, /device:TPU:10, one launch (start us, length us, event | category | flops | bytes accessed | tf_op | source)
XLA Modules:
  0.0 73.5 jit_solution(4152398398347064643)
XLA Ops:
  0.0 69.5 %shard_map.109 = (f32[4,128,1024]{2,1,0:T(8,128)}, bf16[8,4,128,128]{3,2,1,0:T(8,128)(2,1)}) custom-call(bf16[4,128,1024]{2,1,0:T(8,128)(2,1)} %bitcast.9, bf16[1,1024,1024]{2,1,0:T(8,128)(2,1)} %beta_op.1, bf16[1,4,8,128,128]{4,3,2,1,0:T(8,128)(2,1)} %mix_op.1, bf16[8,128,128]{2,1,0:T(8,128)(2,1)} %pair_op.1, s32[8,2,8]{2,1,0:T(2,128)} %bitcast.10, ...), custom_call_target="tpu_custom_call" | custom-call | flops 3221225472 | bytes 6291456 | tf_op jit(solution)/shard_map/pallas_call | solution.py:425
  69.5 4.0 %shard_map.110 = f32[4,128,1024]{2,1,0:T(8,128)} custom-call(f32[4,128,1024]{2,1,0:T(8,128)} %get-tuple-element.7.local, bf16[8,4,128,128]{3,2,1,0:T(8,128)(2,1)} %get-tuple-element.8.back), custom_call_target="tpu_custom_call" | custom-call | tf_op jit(solution)/shard_map/pallas_call | solution.py:472
